TPU v7x, 128 devices: a whole 4x4x4 slice. The times are simulated.
128 devices in a mesh: peer: 32 (over x, y_hi, z), chan: 4 (over y_lo, core).
Axes of the slice: x: 4, y: 4 (y_hi: 2, y_lo: 2; y = y_hi * 2 + y_lo), z: 4, core: 2. Of those that a mesh axis runs over, the one named last changes fastest.
Arguments:
- images: bfloat16 [2, 64, 14, 14, 512], P(None, 'peer', None, None, 'chan'), may hold values from -12 to 12
- cotangent: bfloat16 [2, 32, 4, 14, 14, 512], P(None, 'peer', None, None, None, 'chan'), may hold values from -6 to 6
- image_ids: int32 [2, 32, 4], P(None, 'peer'), may hold values from 0 to 63, as said below
- counts: int32 [2, 32], P(None, 'peer'), may hold values from 1 to 4, 64 in all within a row
- hop_exponents: int32 [2], replicated, may hold values from 0 to 2
- param_mats: float32 [32, 2, 512, 2048], P('peer', None, None, 'chan'), may hold values from -0.25 to 0.25
- param_chans: float32 [32, 54, 512], P('peer', None, 'chan'), may hold values from -3 to 3
- param_bias: float32 [32, 2048], P('peer', 'chan'), may hold values from -3 to 3
- track_mats: float32 [32, 2, 512, 2048], P('peer', None, None, 'chan'), may hold values from -6 to 6
- track_chans: float32 [32, 54, 512], P('peer', None, 'chan'), may hold values from -6 to 6
- track_bias: float32 [32, 2048], P('peer', 'chan'), may hold values from -6 to 6
- grad_mats: float32 [32, 2, 512, 2048], P('peer', None, None, 'chan'), may hold values from -6 to 6
- grad_chans: float32 [32, 54, 512], P('peer', None, 'chan'), may hold values from -6 to 6
- grad_bias: float32 [32, 2048], P('peer', 'chan'), may hold values from -6 to 6
Outputs:
- new_param_mats: float32 [32, 2, 512, 2048], P('peer', None, None, 'chan')
- new_param_chans: float32 [32, 54, 512], P('peer', None, 'chan')
- new_param_bias: float32 [32, 2048], P('peer', 'chan')
- new_track_mats: float32 [32, 2, 512, 2048], P('peer', None, None, 'chan')
- new_track_chans: float32 [32, 54, 512], P('peer', None, 'chan')
- new_track_bias: float32 [32, 2048], P('peer', 'chan')
Inputs may be any that keep to these rules, and one draw needn't show every extreme that they name: `image_ids`: entry s of a worker's list is read only where s is below its count; in each worker's list at most 2 entries name rows of one loader shard (rows b * 2 to (b + 1) * 2 - 1), and in every iteration some list has exactly 2 such entries. `counts`: in every iteration some worker has all 4 entries live.
All inputs are finite; a program needn't handle non-finite values. No bound on the sum of `counts` on one device may be relied on, other than what follows from the above.
Results may differ from a plain program's by a relative error of at most 0.006.
Values may be sent and summed in bfloat16 or wider, within the bound.
A program may use at most 128 MiB of HBM per device.

v0:
```python
import functools

import jax
import jax.numpy as jnp
from jax import lax
from jax.experimental import pallas as pl
from jax.experimental.pallas import tpu as pltpu
from jax.sharding import PartitionSpec as P

KS = 7
TAPS = KS * KS
ITERS = 2
EPS = 1e-06
LEARNING_RATE = 0.01
MESH = pl.DeviceIdType.MESH
F32 = jnp.float32
BF16 = jnp.bfloat16

SIDE = 14
PADW = 16
HALF = SIDE // 2
SLOTS = 4
SROWS = SIDE * PADW
ROWS = SLOTS * SROWS
CW = 128
C = 512
HID = 512
NCHUNK = 8
CROWS = 128
NCHAN = 4
STATW = ROWS + CW


def aligned(value, step):
    return pl.multiple_of(value, step)


def dot(a, b, ca, cb):
    return lax.dot_general(a, b, (((ca,), (cb,)), ((), ())), preferred_element_type=F32)


def terms_of(values, terms):
    parts = []
    for _ in range(terms):
        part = values.astype(BF16)
        parts.append(part)
        values = values - part.astype(F32)
    return parts


def lane_sums(values, terms=2):
    ones = jnp.ones((8, values.shape[1]), BF16)
    total = None
    for part in terms_of(values, terms):
        here = dot(ones, part, 1, 1)
        total = here if total is None else total + here
    return total


def two_rows(first, second):
    row = lax.broadcasted_iota(jnp.int32, (8, first.shape[-1]), 0)
    return jnp.where(row == 0, first, jnp.where(row == 1, second, 0.0))


def two_columns(first, second):
    row = lax.broadcasted_iota(jnp.int32, (16, first.shape[-1]), 0)
    rows = jnp.zeros((16, first.shape[-1]), F32)
    for k, part in enumerate(terms_of(first, 3) + terms_of(second, 3)):
        rows = jnp.where(row == k, part.astype(F32), rows)
    row = lax.broadcasted_iota(jnp.int32, (16, 2 * CW), 0)
    lane = lax.broadcasted_iota(jnp.int32, (16, 2 * CW), 1)
    offset = row - jnp.where(lane < CW, 0, 3)
    pick = jnp.where((offset >= 0) & (offset < 3), 1.0, 0.0)
    both = dot(rows.astype(BF16), pick.astype(BF16), 0, 0)
    return both[:, :CW], both[:, CW:]


def kernel(t, hop, names, *refs):
    r = dict(zip(names, refs))
    first = t == 0
    peer = lax.axis_index("peer")
    chan = lax.axis_index("chan")
    my_z, my_y, my_x = peer % 4, (peer // 4) % 2, peer // 8
    core, side = chan % 2, chan // 2

    def at(new_peer, new_chan):
        return (new_peer, new_chan)

    c_core = side * 2 + 1 - core
    c_side = (1 - side) * 2 + core
    c_diag = (1 - side) * 2 + 1 - core
    d_core, d_side, d_diag = at(peer, c_core), at(peer, c_side), at(peer, c_diag)
    bit = (peer // (2**hop)) % 2
    d_hop = at(peer + (1 - 2 * bit) * (2**hop), chan)
    mine = {"x": my_x, "y": my_y, "z": my_z}
    count_of = {"x": 4, "y": 2, "z": 4}
    stride_of = {"x": 8, "y": 4, "z": 1}
    to, source, line = {}, {}, {}
    for dim, n in count_of.items():
        to[dim] = [(mine[dim] + d) % n for d in range(1, n)]
        source[dim] = [(mine[dim] + n - d) % n for d in range(1, n)]
        line[dim] = [at(peer + (c - mine[dim]) * stride_of[dim], chan) for c in to[dim]]

    counters = {"remote": 0, "local": 0}
    ends = []

    def take(kind, n):
        start = counters[kind]
        counters[kind] += n
        return start

    def remote(src, dst, device, index):
        return pltpu.make_async_remote_copy(
            src_ref=src,
            dst_ref=dst,
            send_sem=r["send"].at[index],
            recv_sem=r["recv"].at[index],
            device_id=device,
            device_id_type=MESH,
        )

    def push(src, dst, device):
        copy = remote(src, dst, device, take("remote", 1))
        copy.start()
        ends.append(copy.wait_send)
        return copy

    def local(src, dst):
        copy = pltpu.make_async_copy(src, dst, r["local"].at[take("local", 1)])
        copy.start()
        return copy

    P2, Y2, G2, F2 = r["P2"], r["Y2"], r["G2"], r["F2"]
    PB, PP, YB, YP, W = r["PB"], r["PP"], r["YB"], r["YP"], r["W"]

    def piece(ref, i):
        return ref.at[i // 4, pl.ds(aligned((i % 4) * CROWS, CROWS), CROWS), :]

    if first:
        G = [[r["G%d%d" % (u, h)] for h in range(2)] for u in range(2)]
        plan = ("yzx", "yxz", "yzx", "yxz") if hop == 2 else ("zyx", "zyx", "yzx", "yzx")
        order = {(u, h): plan[2 * u + h] for u in range(2) for h in range(2)}

        def block(u, h, near, far):
            return G[u][h].at[pl.ds((near * count_of[order[u, h][1]] + far) * 2, 2)]

        def own_block(u, h):
            return block(u, h, mine[order[u, h][0]], mine[order[u, h][1]])

        img_in = {
            (u, h): local(r["images"].at[u, :, pl.ds(h * HALF, HALF)], own_block(u, h))
            for u in range(2)
            for h in range(2)
        }
    p_sem = take("local", NCHUNK)

    def p_load(i):
        return pltpu.make_async_copy(
            piece(r["pm"].at[0], i), piece(P2, i), r["local"].at[p_sem + i]
        )

    def start_p(i, carry):
        p_load(i).start()
        return carry

    lax.fori_loop(0, NCHUNK, start_p, 0)
    CF = r["CF"]
    my_lanes = pl.ds(aligned(chan * CW, CW), CW)
    side_lanes = pl.ds(aligned(c_side * CW, CW), CW)
    cot_in = local(r["cot"].at[t], CF.at[:, my_lanes])
    y_in = local(r["ym"].at[0], Y2)
    g_in = local(r["gm"].at[0], G2)

    count = r["counts"][0, t]

    def valid(s):
        return jnp.where(s < count, 1.0, 0.0).astype(F32)

    inv = 1.0 / jnp.full((1, CW), count.astype(F32))

    if first:
        IDV = r["IDV"]
        lane = lax.broadcasted_iota(jnp.int32, (8, 128), 1)
        row = lax.broadcasted_iota(jnp.int32, (8, 128), 0)
        tile = jnp.zeros((8, 128), jnp.int32)
        for u in range(2):
            for s in range(SLOTS):
                tile = jnp.where((row == u) & (lane == s), r["ids"][u, 0, s], tile)
        IDV[0, my_x] = tile
        IDV[1, my_z] = tile

    barrier = pltpu.get_barrier_semaphore()
    greet = [d_core, d_side, d_diag] + (line["y"] + line["z"] + line["x"] if first else [d_hop])
    for device in greet:
        pl.semaphore_signal(barrier, inc=1, device_id=device, device_id_type=MESH)
    pl.semaphore_wait(barrier, len(greet))

    small = [
        push(r["pc"], r["RPC"], d_hop),
        push(r["pb"], r["RPB"], d_hop),
        push(r["yc"], r["RYC"], d_hop),
        push(r["yb"], r["RYB"], d_hop),
    ]

    fetch = {}
    if first:
        fetch["ids"] = [
            push(IDV.at[k, mine[dim]], IDV.at[k, mine[dim]], d)
            for k, dim in enumerate("xz")
            for d in line[dim]
        ]

    def images_begin(u):
        for h in range(2):
            near, far, _ = order[u, h]
            img_in[u, h].wait()
            own = own_block(u, h)
            fetch["near", u, h] = [push(own, own, d) for d in line[near]]
            fetch["far", u, h] = [push(own, own, d) for d in line[far]]

    def images_second(u):
        for h in range(2):
            near, far, _ = order[u, h]
            for copy, place in zip(fetch["near", u, h], source[near]):
                copy.wait_recv()
                part = block(u, h, place, mine[far])
                fetch["far", u, h] += [push(part, part, d) for d in line[far]]

    def place_of(ident, dim):
        return (ident // (2 * stride_of[dim])) % count_of[dim]

    def images_third(u):
        for h in range(2):
            near, far, last = order[u, h]
            for copy in fetch["far", u, h]:
                copy.wait_recv()
            XS, XR = r["XS"], r["XR%d%d" % (u, h)]

            def wanted(c, s):
                ident = r["IDS"]["xz".index(last), c, u, s]
                row = place_of(ident, near) * count_of[far] + place_of(ident, far)
                return G[u][h][row * 2 + ident % 2]

            fetch["x", u, h] = []
            for j in range(3):
                for s in range(SLOTS):
                    XS[u, h, j, s] = wanted(to[last][j], s)
                fetch["x", u, h].append(push(XS.at[u, h, j], XR.at[mine[last]], line[last][j]))
            for s in range(SLOTS):
                XR[mine[last], s] = wanted(mine[last], s)

    def images_end(u):
        for h in range(2):
            for copy in fetch["x", u, h]:
                copy.wait_recv()

    def picked(u, h, s):
        return r["XR%d%d" % (u, h)][place_of(r["ids"][u, 0, s], order[u, h][2]), s]

    if first:
        images_begin(0)

    p_send = take("remote", NCHUNK)

    def p_copy(i):
        return remote(piece(PB, i), piece(PP, i), d_hop, p_send + i)

    def rows_of(i):
        return (i // 4, pl.ds(aligned((i % 4) * CROWS, CROWS), CROWS), slice(None))

    def send_p(i, carry):
        p_load(i).wait()
        PB[rows_of(i)] = P2[rows_of(i)].astype(BF16)
        p_copy(i).start()
        return carry

    lax.fori_loop(0, NCHUNK, send_p, 0)

    r["XP"][...] = jnp.zeros_like(r["XP"])
    cot_in.wait()
    cot_sum = jnp.zeros((1, CW), F32)
    for s in range(SLOTS):
        rows = slice(s * SROWS, (s + 1) * SROWS)
        live = CF[rows, my_lanes].astype(F32) * valid(s)
        CF[rows, my_lanes] = live.astype(BF16)
        cot_sum = cot_sum + jnp.sum(live, 0, keepdims=True)
    cot_core = push(CF.at[:, my_lanes], CF.at[:, my_lanes], d_core)
    cot_side = push(CF.at[:, my_lanes], CF.at[:, my_lanes], d_side)

    for copy in small:
        copy.wait_recv()
    qc, qb = r["qc"], r["qb"]
    qc[...] = 0.5 * (r["pc"][...] + r["RPC"][...]) - LEARNING_RATE * r["yc"][...]
    qb[...] = 0.5 * (r["pb"][...] + r["RPB"][...]) - LEARNING_RATE * r["yb"][...]

    def chan_row(k):
        return qc[k]

    if first:
        images_second(0)
        for copy in fetch["ids"]:
            copy.wait_recv()
        ids_in = local(IDV, r["IDS"])
        ids_in.wait()
        images_third(0)
        images_begin(1)
        images_end(0)

    XP, SH, X = r["XP"], r["SH"], r["X"]
    for s in range(SLOTS):
        for h in range(2):
            image = picked(0, h, s) if first else r["picked"][s, h * HALF : (h + 1) * HALF]
            top = 3 + h * HALF
            XP[s, top : top + HALF, 3 : 3 + PADW, :] = image.astype(F32) * valid(s)

    def shift(s, carry):
        for v in range(KS):
            SH[v, s] = XP[s, :, v : v + PADW, :]
        return carry

    lax.fori_loop(0, SLOTS, shift, 0)

    def conv_slot(s, carry):
        def column(v, acc):
            for u in range(KS):
                acc = acc + SH[v, s, u : u + SIDE] * qc[u * KS + v]
            return acc

        acc = lax.fori_loop(0, KS, column, jnp.zeros((SIDE, PADW, CW), F32))
        X[pl.ds(aligned(s * SROWS, SROWS), SROWS), :] = acc.reshape(SROWS, CW) + chan_row(TAPS)
        return carry

    lax.fori_loop(0, SLOTS, conv_slot, 0)

    STR = r["STR"]
    conv_out = X[...]
    mean_here = jnp.sum(conv_out, 1, keepdims=True) * (1.0 / CW)
    centred = conv_out - mean_here
    mean_row = lane_sums(conv_out, 3) * (1.0 / CW)
    STR[chan, :, 0:ROWS] = two_rows(mean_row, lane_sums(centred * centred))
    STR[chan, :, ROWS:STATW] = jnp.broadcast_to(chan_row(TAPS + 4), (8, CW))
    stats = [push(STR.at[chan], STR.at[chan], d) for d in (d_core, d_side, d_diag)]
    cot_side.wait_recv()
    cot_far = push(CF.at[:, side_lanes], CF.at[:, side_lanes], d_core)
    for copy in stats:
        copy.wait_recv()
    means = [STR[j, 0:1, 0:ROWS] for j in range(NCHAN)]
    mean = (means[0] + means[1] + means[2] + means[3]) * 0.25
    squares = STR[0, 1:2, 0:ROWS] + STR[1, 1:2, 0:ROWS] + STR[2, 1:2, 0:ROWS] + STR[3, 1:2, 0:ROWS]
    for j in range(NCHAN):
        squares = squares + CW * (means[j] - mean) * (means[j] - mean)
    deviation = lax.rsqrt(squares * (1.0 / C) + EPS)
    mean_col, inv_col = two_columns(mean, deviation)
    r["INV"][...] = inv_col
    xhat = (X[...] - mean_col) * inv_col
    X[...] = xhat
    NF = r["NF"]
    NF[:, my_lanes] = (xhat * chan_row(TAPS + 1) + chan_row(TAPS + 2)).astype(BF16)

    na, nb, nc = take("remote", SLOTS), take("remote", SLOTS), take("remote", SLOTS)

    def slot_rows(s):
        return pl.ds(aligned(s * SROWS, SROWS), SROWS)

    def norm_core(s):
        part = NF.at[slot_rows(s), my_lanes]
        return remote(part, part, d_core, na + s)

    def norm_side(s):
        part = NF.at[slot_rows(s), my_lanes]
        return remote(part, part, d_side, nb + s)

    def norm_far(s):
        part = NF.at[slot_rows(s), side_lanes]
        return remote(part, part, d_core, nc + s)

    def norm_send(s, carry):
        norm_side(s).start()
        norm_core(s).start()
        return carry

    lax.fori_loop(0, SLOTS, norm_send, 0)

    if first:
        images_second(1)

    cot_core.wait_recv()
    cot_far.wait_recv()
    DB = r["DB"]
    for j in range(NCHAN):
        lanes = slice(j * CW, (j + 1) * CW)
        factor = inv * STR[j, 0:1, ROWS:STATW]
        DB[:, lanes] = (CF[:, lanes].astype(F32) * factor).astype(BF16)

    y_in.wait()

    def mix(i, carry):
        p_copy(i).wait_recv()
        q = 0.5 * (P2[rows_of(i)] + PP[rows_of(i)].astype(F32)) - LEARNING_RATE * Y2[rows_of(i)]
        P2[rows_of(i)] = q
        W[rows_of(i)] = q.astype(BF16)
        return carry

    lax.fori_loop(0, NCHUNK, mix, 0)
    q_out = local(P2, r["qm"].at[0])

    y_send = take("remote", NCHUNK)

    def y_copy(i):
        return remote(piece(YB, i), piece(YP, i), d_hop, y_send + i)

    def send_y(i, carry):
        YB[rows_of(i)] = Y2[rows_of(i)].astype(BF16)
        y_copy(i).start()
        return carry

    if hop != 2:
        lax.fori_loop(0, NCHUNK, send_y, 0)

    if first:
        images_third(1)

    ACT, DH, DP, R1, S2, R2, DN = (r[n] for n in ("ACT", "DH", "DP", "R1", "S2", "R2", "DN"))
    r1, r2 = take("remote", 2 * SLOTS), take("remote", SLOTS)

    def near_copy(s, b):
        lanes = pl.ds(aligned((b * 2 + 1 - core) * CW, CW), CW)
        return remote(DP.at[slot_rows(s), lanes], R1.at[b, slot_rows(s)], d_core, r1 + 2 * s + b)

    def far_copy(s):
        return remote(S2.at[slot_rows(s)], R2.at[slot_rows(s)], d_side, r2 + s)

    GB = r["GB"]
    GB[...] = jnp.zeros_like(GB)

    def slot_step(step, carry):
        if hop == 2:
            send_y(step, carry)

        @pl.when(step < SLOTS)
        def _():
            norm_side(step).wait_recv()
            norm_far(step).start()

        @pl.when((step > 0) & (step <= SLOTS))
        def _():
            s = step - 1
            norm_core(s).wait_recv()
            norm_far(s).wait_recv()
            rows = slot_rows(s)
            hidden = dot(NF[rows, :], W[0], 1, 0) + qb[...]
            cdf = 0.5 * (1.0 + lax.erf(hidden * 0.7071067811865476))
            density = jnp.exp(-0.5 * hidden * hidden) * 0.3989422804014327
            ACT[rows, :] = (hidden * cdf).astype(BF16)
            slope = cdf + hidden * density
            dhidden = dot(DB[rows, :], W[1], 1, 0) * slope
            GB[...] += jnp.sum(dhidden, 0, keepdims=True)
            low = dhidden.astype(BF16)
            DH[rows, :] = low
            DP[rows, :] = dot(low, W[0], 1, 1)
            near_copy(s, 0).start()
            near_copy(s, 1).start()

        @pl.when(step > 1)
        def _():
            s = step - 2
            rows = slot_rows(s)
            near_copy(s, 0).wait_recv()
            near_copy(s, 1).wait_recv()
            S2[rows, :] = (DP[rows, side_lanes] + R1[1 - side, rows, :]).astype(BF16)
            far_copy(s).start()
            DN[rows, :] = DP[rows, my_lanes] + R1[side, rows, :]

        return carry

    lax.fori_loop(0, SLOTS + 2, slot_step, 0)
    if hop == 2:
        lax.fori_loop(SLOTS + 2, NCHUNK, send_y, 0)

    BS, BR, GS = r["BS"], r["BR"], r["GS"]

    def scale_part(j, carry):
        lanes = pl.ds(aligned(j * CW, CW), CW)
        rows = pl.ds(aligned(j * CW, CW), CW)
        pair = dot(CF[:, lanes], ACT[...], 0, 0)
        weight = W[1, rows, :].astype(F32)
        GS[j] = lane_sums(pair * weight)
        return carry

    lax.fori_loop(0, NCHAN, scale_part, 0)

    def far_wait(s, carry):
        far_copy(s).wait_recv()
        return carry

    lax.fori_loop(0, SLOTS, far_wait, 0)
    dnormed = DN[...] + R2[...].astype(F32)
    DN[...] = dnormed
    xhat = X[...]
    dxhat = dnormed * chan_row(TAPS + 1)
    sums = two_rows(lane_sums(dxhat), lane_sums(dxhat * xhat))
    for j in range(NCHAN):
        BS[j, :, 0:ROWS] = sums
        BS[j, :, ROWS:STATW] = GS[j]
    BR[chan] = BS[chan]
    back = [
        push(BS.at[c], BR.at[chan], d)
        for c, d in ((c_core, d_core), (c_side, d_side), (c_diag, d_diag))
    ]

    def mats_part(j, carry):
        lanes = pl.ds(aligned(j * CW, CW), CW)
        F2[0, lanes, :] = dot(NF[:, lanes], DH[...], 0, 0)
        F2[1, lanes, :] = dot(DB[:, lanes], ACT[...], 0, 0)
        return carry

    lax.fori_loop(0, NCHAN, mats_part, 0)
    if first:
        f_out = local(F2, r["fm"].at[0])

    for copy in back:
        copy.wait_recv()
    totals = BR[0] + BR[1] + BR[2] + BR[3]
    mean_a, mean_b = two_columns(
        totals[0:1, 0:ROWS] * (1.0 / C), totals[1:2, 0:ROWS] * (1.0 / C)
    )
    dnormed = DN[...]
    xhat = X[...]
    dconv = (dnormed * chan_row(TAPS + 1) - mean_a - xhat * mean_b) * r["INV"][...]
    DC, FC = r["DC"], r["FC"]
    DC[...] = dconv.reshape(SLOTS, SIDE, PADW, CW)
    FC[TAPS] = jnp.sum(dconv, 0, keepdims=True)
    FC[TAPS + 1] = jnp.sum(dnormed * xhat, 0, keepdims=True)
    FC[TAPS + 2] = jnp.sum(dnormed, 0, keepdims=True)
    FC[TAPS + 3] = chan_row(TAPS + 4) * inv * cot_sum
    FC[TAPS + 4] = inv * (totals[0:1, ROWS:STATW] + chan_row(TAPS + 3) * cot_sum)

    def tap_column(v, carry):
        def over(s, accs):
            grad = DC[s]
            return tuple(
                accs[u] + jnp.sum(SH[v, s, u : u + SIDE] * grad, 0) for u in range(KS)
            )

        accs = lax.fori_loop(0, SLOTS, over, tuple(jnp.zeros((PADW, CW), F32) for _ in range(KS)))
        for u in range(KS):
            FC[u * KS + v] = jnp.sum(accs[u], 0, keepdims=True)
        return carry

    lax.fori_loop(0, KS, tap_column, 0)

    fresh = FC[...]
    r["new_yc"][...] = 0.5 * (r["yc"][...] + r["RYC"][...]) + fresh - r["gc"][...]
    r["new_yb"][...] = 0.5 * (r["yb"][...] + r["RYB"][...]) + GB[...] - r["gb"][...]
    if first:
        r["fc"][...] = fresh
        r["fb"][...] = GB[...]
        images_end(1)
        for s in range(SLOTS):
            for h in range(2):
                r["picked_next"][s, h * HALF : (h + 1) * HALF] = picked(1, h, s)

    g_in.wait()
    out_sem = take("local", NCHUNK)

    def y_out(i):
        return pltpu.make_async_copy(
            piece(Y2, i), piece(r["new_ym"].at[0], i), r["local"].at[out_sem + i]
        )

    def track(i, carry):
        y_copy(i).wait_recv()
        at_i = rows_of(i)
        Y2[at_i] = 0.5 * (Y2[at_i] + YP[at_i].astype(F32)) + F2[at_i] - G2[at_i]
        y_out(i).start()
        return carry

    lax.fori_loop(0, NCHUNK, track, 0)

    def swaps_end(i, carry):
        p_copy(i).wait_send()
        y_copy(i).wait_send()
        y_out(i).wait()
        return carry

    lax.fori_loop(0, NCHUNK, swaps_end, 0)

    def slots_end(s, carry):
        norm_core(s).wait_send()
        norm_side(s).wait_send()
        norm_far(s).wait_send()
        near_copy(s, 0).wait_send()
        near_copy(s, 1).wait_send()
        far_copy(s).wait_send()
        return carry

    lax.fori_loop(0, SLOTS, slots_end, 0)
    for wait in ends:
        wait()
    q_out.wait()
    if first:
        f_out.wait()


def iteration(t, hop, state, images, cot, ids, counts):
    first = t == 0
    pm, pc, pb, ym, yc, yb, gm, gc, gb = state
    hbm = pl.BlockSpec(memory_space=pl.ANY)
    vmem = pl.BlockSpec(memory_space=pltpu.VMEM)
    smem = pl.BlockSpec(memory_space=pltpu.SMEM)
    ins = [("images", images, hbm), ("ids", ids, smem)] if first else [("picked", images, vmem)]
    ins += [("counts", counts, smem), ("cot", cot, hbm)]
    ins += [("pm", pm, hbm), ("pc", pc, vmem), ("pb", pb, vmem)]
    ins += [("ym", ym, hbm), ("yc", yc, vmem), ("yb", yb, vmem)]
    ins += [("gm", gm, hbm), ("gc", gc, vmem), ("gb", gb, vmem)]
    outs = [("qm", pm, hbm), ("qc", pc, vmem), ("qb", pb, vmem)]
    outs += [("new_ym", ym, hbm), ("new_yc", yc, vmem), ("new_yb", yb, vmem)]
    if first:
        outs += [("fm", gm, hbm), ("fc", gc, vmem), ("fb", gb, vmem)]
        outs += [("picked_next", jax.ShapeDtypeStruct((SLOTS, SIDE, PADW, CW), BF16), vmem)]
    V = pltpu.VMEM
    mats = (2, C, HID)
    half = (HALF, PADW, CW)
    scratch = {n: V(mats, F32) for n in ("P2", "Y2", "G2", "F2")}
    scratch |= {n: V(mats, BF16) for n in ("PB", "PP", "YB", "YP", "W")}
    scratch |= {n: V((ROWS, C), BF16) for n in ("NF", "CF", "DB", "ACT", "DH")}
    scratch |= {n: V((ROWS, CW), F32) for n in ("X", "INV", "DN")}
    scratch |= {n: V((ROWS, CW), BF16) for n in ("S2", "R2")}
    scratch |= {n: V((SLOTS, SIDE, PADW, CW), F32) for n in ("DC",)}
    scratch |= {n: V((NCHAN, 8, STATW), F32) for n in ("STR", "BS", "BR")}
    scratch |= {n: V((TAPS + 5, 1, CW), F32) for n in ("RPC", "RYC", "FC")}
    scratch |= {n: V((1, HID), F32) for n in ("RPB", "RYB", "GB")}
    scratch |= {
        "DP": V((ROWS, C), F32),
        "R1": V((2, ROWS, CW), F32),
        "GS": V((NCHAN, 8, CW), F32),
        "XP": V((SLOTS, SIDE + 6, 24, CW), F32),
        "SH": V((KS, SLOTS, SIDE + 6, PADW, CW), F32),
        "send": pltpu.SemaphoreType.DMA((128,)),
        "recv": pltpu.SemaphoreType.DMA((128,)),
        "local": pltpu.SemaphoreType.DMA((32,)),
    }
    if first:
        for u in range(2):
            for h in range(2):
                scratch["G%d%d" % (u, h)] = V((16,) + half, BF16)
                scratch["XR%d%d" % (u, h)] = V((4, SLOTS) + half, BF16)
        scratch |= {
            "XS": V((2, 2, 3, SLOTS) + half, BF16),
            "IDV": V((2, 4, 8, 128), jnp.int32),
            "IDS": pltpu.SMEM((2, 4, 8, 128), jnp.int32),
        }
    names = [n for n, _, _ in ins] + [n for n, _, _ in outs] + list(scratch)
    return pl.pallas_call(
        functools.partial(kernel, t, hop, names),
        out_shape=[jax.ShapeDtypeStruct(a.shape, a.dtype) for _, a, _ in outs],
        in_specs=[s for _, _, s in ins],
        out_specs=[s for _, _, s in outs],
        scratch_shapes=list(scratch.values()),
        compiler_params=pltpu.CompilerParams(
            collective_id=t * 3 + hop,
            has_side_effects=True,
            vmem_limit_bytes=58 * 1024 * 1024,
        ),
    )(*[a for _, a, _ in ins])


def copies(*refs):
    n = len(refs) // 2
    started = [pltpu.make_async_copy(refs[i], refs[n + i], refs[2 * n].at[i]) for i in range(n)]
    for copy in started:
        copy.start()
    for copy in started:
        copy.wait()


def handed_on(values):
    hbm = pl.BlockSpec(memory_space=pl.ANY)
    return pl.pallas_call(
        copies,
        out_shape=[jax.ShapeDtypeStruct(a.shape, a.dtype) for a in values],
        in_specs=[hbm] * len(values),
        out_specs=[hbm] * len(values),
        scratch_shapes=[pltpu.SemaphoreType.DMA((len(values),))],
    )(*values)


def on_device(images, cotangent, image_ids, counts, hop_exponents, *state):
    def padded(maps):
        return jnp.pad(maps, ((0, 0), (0, 0), (0, 0), (0, PADW - SIDE), (0, 0)))

    images = padded(images)
    cot = padded(cotangent[:, 0]).reshape(ITERS, ROWS, CW)
    counts = counts.T

    def turned(values):
        return tuple(a.transpose(1, 0, 2) if i % 3 == 1 else a for i, a in enumerate(values))

    def branch(t, hop):
        def run(operands):
            source, state = operands
            return iteration(t, hop, state, source, cot, image_ids, counts)

        return run

    def step(t, source, state):
        return lax.switch(
            hop_exponents[t], [branch(t, hop) for hop in range(3)], (source, state)
        )

    out = step(0, images, turned(state))
    return turned(handed_on(step(1, out[9], tuple(out[:9]))))


def solution(mesh):
    mats, chans, bias = P("peer", None, None, "chan"), P("peer", None, "chan"), P("peer", "chan")
    in_specs = (
        P(None, "peer", None, None, "chan"),
        P(None, "peer", None, None, None, "chan"),
        P(None, "peer", None),
        P(None, "peer"),
        P(),
    ) + (mats, chans, bias) * 3
    return jax.shard_map(
        on_device, mesh=mesh, in_specs=in_specs, out_specs=(mats, chans, bias) * 2, check_vma=False
    )
```

profile of v0, /device:TPU:1, one launch (start us, length us, event | category | flops | bytes accessed | tf_op | source)
XLA Modules:
  0.0 239.8 jit_solution(1669487162291394415)
XLA Ops:
  0.6 0.0 copy-start.6
  0.6 0.0 copy-start.3
  0.7 0.0 copy-start.5
  0.7 0.0 copy-start.2
  0.7 0.0 copy-start.4
  0.7 0.0 copy-start.1
  0.7 0.0 copy-start
  0.7 0.0 copy-start.7
  0.7 0.0 copy-start.8
  0.7 1.4 fusion
  3.4 1.0 copy.20
  4.5 1.1 copy.22
  5.5 0.1 pad.9.clone
  5.6 0.0 copy-done.6
  5.6 0.0 copy-done.3
  5.7 0.0 copy-done.5
  5.7 0.0 copy-done.2
  5.7 0.0 copy-done.4
  5.7 0.0 copy-done.1
  5.7 0.0 copy-done
  5.7 0.0 copy-done.7
  5.7 0.0 copy-done.8
  5.7 91.1 %conditional.2 = ((f32[1,2,512,512]{3,2,1,0:T(8,128)}, f32[54,1,128]{2,1,0:T(1,128)S(1)}, f32[1,512]{1,0:T(1,128)S(1)}, f32[1,2,512,512]{3,2,1,0:T(8,128)}, f32[...) conditional(s32[]{:T(128)} %bitcast.1, ...), branch_computations={%region_0.1_spmd, %region_1.2_spmd, %region_2.3_spmd} | conditional | bytes 8 | solution.py:707
  5.9 90.7 %branch_1_fun.2 = (f32[1,2,512,512]{3,2,1,0:T(8,128)}, f32[54,1,128]{2,1,0:T(1,128)S(1)}, f32[1,512]{1,0:T(1,128)S(1)}, f32[1,2,512,512]{3,2,1,0:T(8,128)}, f32[...) custom-call(bf16[2,2,14,16,128]{4,3,2,1,0:T(8,128)(2,1)S(1)} %get-tu, ...), custom_call_target="tpu_custom_call" | custom-call | tf_op jit(solution)/shard_map/cond/branch_1_fun/pallas_call | solution.py:654
  96.9 78.0 %conditional.3 = ((f32[1,2,512,512]{3,2,1,0:T(8,128)S(1)}, f32[54,1,128]{2,1,0:T(1,128)S(1)}, f32[1,512]{1,0:T(1,128)S(1)}, f32[1,2,512,512]{3,2,1,0:T(8,128)}, ...) conditional(s32[]{:T(128)} %bitcast, (bf16[4,14,16,128]{3,2,1,0:T(8,128)(2,1)S(1)}, ...), branch_computations={%region_3.4_spmd, %region_4.5_spmd, %region_5.6_spmd} | conditional | bytes 8 | solution.py:707
  97.2 77.4 %branch_2_fun.3 = (f32[1,2,512,512]{3,2,1,0:T(8,128)S(1)}, f32[54,1,128]{2,1,0:T(1,128)S(1)}, f32[1,512]{1,0:T(1,128)S(1)}, f32[1,2,512,512]{3,2,1,0:T(8,128)}, ...) custom-call(bf16[4,14,16,128]{3,2,1,0:T(8,128)(2,1)S(1)} %get-tuple-element.213.refs_0_, ...), custom_call_target="tpu_custom_call" | custom-call | tf_op jit(solution)/shard_map/cond/branch_2_fun/pallas_call | solution.py:654
  174.9 64.7 %shard_map.181 = (f32[1,2,512,512]{3,2,1,0:T(8,128)}, f32[54,1,128]{2,1,0:T(1,128)}, f32[1,512]{1,0:T(1,128)}, f32[1,2,512,512]{3,2,1,0:T(8,128)}, f32[54,1,128]{2,1,0:T(1,128)}, /*index=5*/f32[1,512]{1,0:T(1,128)}) custom-call(f32[1,2,512,512]{3,2,1,0:T(8,128)S(1)} %get-tuple-element.263.refs_0_, f32[54,1,128]{2,1,0:T(1,128)S(1)} %get-tuple-element.264.refs_1_, ...), custom_call_target="tpu_custom_call" | custom-call | tf_op jit(solution)/shard_map/pallas_call | solution.py:679
  (1 shorter events, 0.0 us)
Async XLA Ops:
  0.6 5.0 %copy-start.6 = (f32[1,512]{1,0:T(1,128)S(1)}, f32[1,512]{1,0:T(1,128)}, u32[]{:S(2)}) copy-start(f32[1,512]{1,0:T(1,128)} %param.33) | copy-start | bytes 6148
  0.6 5.0 %copy-start.3 = (f32[1,54,128]{2,0,1:T(1,128)S(1)}, f32[1,54,128]{2,0,1:T(1,128)}, u32[]{:S(2)}) copy-start(f32[1,54,128]{2,0,1:T(1,128)} %param.32) | copy-start | bytes 82948
  0.7 5.0 %copy-start.5 = (f32[1,512]{1,0:T(1,128)S(1)}, f32[1,512]{1,0:T(1,128)}, u32[]{:S(2)}) copy-start(f32[1,512]{1,0:T(1,128)} %param.30) | copy-start | bytes 6148
  0.7 5.0 %copy-start.2 = (f32[1,54,128]{2,0,1:T(1,128)S(1)}, f32[1,54,128]{2,0,1:T(1,128)}, u32[]{:S(2)}) copy-start(f32[1,54,128]{2,0,1:T(1,128)} %param.29) | copy-start | bytes 82948
  0.7 5.0 %copy-start.4 = (f32[1,512]{1,0:T(1,128)S(1)}, f32[1,512]{1,0:T(1,128)}, u32[]{:S(2)}) copy-start(f32[1,512]{1,0:T(1,128)} %param.27) | copy-start | bytes 6148
  0.7 5.0 %copy-start.1 = (f32[1,54,128]{2,0,1:T(1,128)S(1)}, f32[1,54,128]{2,0,1:T(1,128)}, u32[]{:S(2)}) copy-start(f32[1,54,128]{2,0,1:T(1,128)} %param.26) | copy-start | bytes 82948
  0.7 5.0 %copy-start = (f32[1,2,512,512]{3,2,1,0:T(8,128)S(1)}, f32[1,2,512,512]{3,2,1,0:T(8,128)}, u32[]{:S(2)}) copy-start(f32[1,2,512,512]{3,2,1,0:T(8,128)} %param.25) | copy-start | bytes 6291460
  0.7 5.0 %copy-start.7 = (s32[2,1]{0,1:T(1,128)S(1)}, s32[2,1]{0,1:T(1,128)}, u32[]{:S(2)}) copy-start(s32[2,1]{0,1:T(1,128)} %param.23) | copy-start | bytes 28
  0.7 5.0 %copy-start.8 = (s32[2,1,4]{2,1,0:T(1,128)S(1)}, s32[2,1,4]{2,1,0:T(1,128)}, u32[]{:S(2)}) copy-start(s32[2,1,4]{2,1,0:T(1,128)} %param.22) | copy-start | bytes 100
where the time goes:
time: 240 us
  Pallas kernels  233 us (97%)
  local copies, waits for them, and re-layouts  3.62 us (2%)
    pallas_call x2, Pallas kernels, iteration(): pl.pallas_call(functools.partial(kernel, t, hop, names), out_shape=[jax.S...  168 us
    pallas_call x1, Pallas kernels, handed_on(): pl.pallas_call(copies, out_shape=[jax.ShapeDtypeStruct(a.shape, a.dtype)...  64.7 us

commit v1 on v0

--- a/solution.py
+++ b/solution.py
@@ -138,8 +138,8 @@
 
     if first:
         G = [[r["G%d%d" % (u, h)] for h in range(2)] for u in range(2)]
-        plan = ("yzx", "yxz", "yzx", "yxz") if hop == 2 else ("zyx", "zyx", "yzx", "yzx")
-        order = {(u, h): plan[2 * u + h] for u in range(2) for h in range(2)}
+        plan = ("yzx", "yxz") if hop == 2 else ("zyx", "zyx")
+        order = {(u, h): plan[h] for u in range(2) for h in range(2)}
 
         def block(u, h, near, far):
             return G[u][h].at[pl.ds((near * count_of[order[u, h][1]] + far) * 2, 2)]
@@ -303,8 +303,8 @@
         ids_in = local(IDV, r["IDS"])
         ids_in.wait()
         images_third(0)
+        images_end(0)
         images_begin(1)
-        images_end(0)
 
     XP, SH, X = r["XP"], r["SH"], r["X"]
     for s in range(SLOTS):
@@ -417,9 +417,6 @@
     if hop != 2:
         lax.fori_loop(0, NCHUNK, send_y, 0)
 
-    if first:
-        images_third(1)
-
     ACT, DH, DP, R1, S2, R2, DN = (r[n] for n in ("ACT", "DH", "DP", "R1", "S2", "R2", "DN"))
     r1, r2 = take("remote", 2 * SLOTS), take("remote", SLOTS)
 
@@ -488,6 +485,9 @@
         return carry
 
     lax.fori_loop(0, NCHAN, scale_part, 0)
+
+    if first:
+        images_third(1)
 
     def far_wait(s, carry):
         far_copy(s).wait_recv()
@@ -665,23 +665,47 @@
     )(*[a for _, a, _ in ins])
 
 
-def copies(*refs):
-    n = len(refs) // 2
-    started = [pltpu.make_async_copy(refs[i], refs[n + i], refs[2 * n].at[i]) for i in range(n)]
-    for copy in started:
+def copies(n, *refs):
+    arrays, results, held, (sem_in, sem_out) = refs[:n], refs[n : 2 * n], refs[2 * n : 3 * n], refs[3 * n :]
+
+    def pieces(k):
+        return [(0, i) for i in range(2)] if k % 3 == 0 else [()]
+
+    def pick(ref, index):
+        return ref.at[index] if index else ref
+
+    moves = []
+    for k in range(n):
+        for index in pieces(k):
+            moves.append((k, index, len(moves)))
+    into = [
+        pltpu.make_async_copy(pick(arrays[k], i), pick(held[k], i), sem_in.at[m])
+        for k, i, m in moves
+    ]
+    out = [
+        pltpu.make_async_copy(pick(held[k], i), pick(results[k], i), sem_out.at[m])
+        for k, i, m in moves
+    ]
+    for copy in into:
         copy.start()
-    for copy in started:
+    for first, second in zip(into, out):
+        first.wait()
+        second.start()
+    for copy in out:
         copy.wait()
 
 
 def handed_on(values):
+    n = len(values)
     hbm = pl.BlockSpec(memory_space=pl.ANY)
     return pl.pallas_call(
-        copies,
+        functools.partial(copies, n),
         out_shape=[jax.ShapeDtypeStruct(a.shape, a.dtype) for a in values],
-        in_specs=[hbm] * len(values),
-        out_specs=[hbm] * len(values),
-        scratch_shapes=[pltpu.SemaphoreType.DMA((len(values),))],
+        in_specs=[hbm] * n,
+        out_specs=[hbm] * n,
+        scratch_shapes=[pltpu.VMEM(a.shape, a.dtype) for a in values]
+        + [pltpu.SemaphoreType.DMA((n + 2,))] * 2,
+        compiler_params=pltpu.CompilerParams(vmem_limit_bytes=16 * 1024 * 1024),
     )(*values)
 
 

time: 240 us -> 154 us (0.64)
  Pallas kernels: 233 us -> 146 us
    pallas_call x1, Pallas kernels: 64.7 us -> 3.6 us  [handed_on(): pl.pallas_call(functools.partial(copies, n), out_shape=[jax.ShapeDtypeStr...]
    pallas_call x2, Pallas kernels: 168 us -> 143 us  [iteration(): pl.pallas_call(functools.partial(kernel, t, hop, names), out_shape=[jax.S...]
where the time goes in v1:
time: 154 us; the launch traced here: 153 us
  Pallas kernels  146 us (95%)
  local copies, waits for them, and re-layouts  3.62 us (2%)
  between operations  2.34 us (2%)
    pallas_call x2, Pallas kernels, iteration(): pl.pallas_call(functools.partial(kernel, t, hop, names), out_shape=[jax.S...  143 us
    pallas_call x1, Pallas kernels, handed_on(): pl.pallas_call(functools.partial(copies, n), out_shape=[jax.ShapeDtypeStr...  3.6 us

profile of v1, /device:TPU:1, one launch (start us, length us, event | category | flops | bytes accessed | tf_op | source)
XLA Modules:
  0.0 153.3 jit_solution(6663044263560071494)
XLA Ops:
  0.6 0.0 copy-start.6
  0.6 0.0 copy-start.3
  0.7 0.0 copy-start.5
  0.7 0.0 copy-start.2
  0.7 0.0 copy-start.4
  0.7 0.0 copy-start.1
  0.7 0.0 copy-start
  0.7 0.0 copy-start.7
  0.7 0.0 copy-start.8
  0.7 1.4 fusion
  3.4 1.0 copy.20
  4.5 1.1 copy.22
  5.5 0.1 pad.9.clone
  5.6 0.0 copy-done.6
  5.6 0.0 copy-done.3
  5.7 0.0 copy-done.5
  5.7 0.0 copy-done.2
  5.7 0.0 copy-done.4
  5.7 0.0 copy-done.1
  5.7 0.0 copy-done
  5.7 0.0 copy-done.7
  5.7 0.0 copy-done.8
  5.7 86.0 %conditional.2 = ((f32[1,2,512,512]{3,2,1,0:T(8,128)}, f32[54,1,128]{2,1,0:T(1,128)S(1)}, f32[1,512]{1,0:T(1,128)S(1)}, f32[1,2,512,512]{3,2,1,0:T(8,128)}, f32[...) conditional(s32[]{:T(128)} %bitcast.1, ...), branch_computations={%region_0.1_spmd, %region_1.2_spmd, %region_2.3_spmd} | conditional | bytes 8 | solution.py:731
  5.9 85.6 %branch_2_fun.2 = (f32[1,2,512,512]{3,2,1,0:T(8,128)}, f32[54,1,128]{2,1,0:T(1,128)S(1)}, f32[1,512]{1,0:T(1,128)S(1)}, f32[1,2,512,512]{3,2,1,0:T(8,128)}, f32[...) custom-call(bf16[2,2,14,16,128]{4,3,2,1,0:T(8,128)(2,1)S(1)} %get-tu, ...), custom_call_target="tpu_custom_call" | custom-call | tf_op jit(solution)/shard_map/cond/branch_2_fun/pallas_call | solution.py:654
  91.7 57.7 %conditional.3 = ((f32[1,2,512,512]{3,2,1,0:T(8,128)S(1)}, f32[54,1,128]{2,1,0:T(1,128)S(1)}, f32[1,512]{1,0:T(1,128)S(1)}, f32[1,2,512,512]{3,2,1,0:T(8,128)}, ...) conditional(s32[]{:T(128)} %bitcast, (bf16[4,14,16,128]{3,2,1,0:T(8,128)(2,1)S(1)}, ...), branch_computations={%region_3.4_spmd, %region_4.5_spmd, %region_5.6_spmd} | conditional | bytes 8 | solution.py:731
  91.8 57.1 %branch_1_fun.3 = (f32[1,2,512,512]{3,2,1,0:T(8,128)S(1)}, f32[54,1,128]{2,1,0:T(1,128)S(1)}, f32[1,512]{1,0:T(1,128)S(1)}, f32[1,2,512,512]{3,2,1,0:T(8,128)}, ...) custom-call(bf16[4,14,16,128]{3,2,1,0:T(8,128)(2,1)S(1)} %get-tuple-element.201.refs_0_, ...), custom_call_target="tpu_custom_call" | custom-call | tf_op jit(solution)/shard_map/cond/branch_1_fun/pallas_call | solution.py:654
  149.4 3.6 %shard_map.181 = (f32[1,2,512,512]{3,2,1,0:T(8,128)}, f32[54,1,128]{2,1,0:T(1,128)}, f32[1,512]{1,0:T(1,128)}, f32[1,2,512,512]{3,2,1,0:T(8,128)}, f32[54,1,128]{2,1,0:T(1,128)}, /*index=5*/f32[1,512]{1,0:T(1,128)}) custom-call(f32[1,2,512,512]{3,2,1,0:T(8,128)S(1)} %get-tuple-element.263.refs_0_, f32[54,1,128]{2,1,0:T(1,128)S(1)} %get-tuple-element.264.refs_1_, ...), custom_call_target="tpu_custom_call" | custom-call | tf_op jit(solution)/shard_map/pallas_call | solution.py:701
  (1 shorter events, 0.0 us)
Async XLA Ops:
  0.6 5.0 %copy-start.6 = (f32[1,512]{1,0:T(1,128)S(1)}, f32[1,512]{1,0:T(1,128)}, u32[]{:S(2)}) copy-start(f32[1,512]{1,0:T(1,128)} %param.33) | copy-start | bytes 6148
  0.6 5.0 %copy-start.3 = (f32[1,54,128]{2,0,1:T(1,128)S(1)}, f32[1,54,128]{2,0,1:T(1,128)}, u32[]{:S(2)}) copy-start(f32[1,54,128]{2,0,1:T(1,128)} %param.32) | copy-start | bytes 82948
  0.7 5.0 %copy-start.5 = (f32[1,512]{1,0:T(1,128)S(1)}, f32[1,512]{1,0:T(1,128)}, u32[]{:S(2)}) copy-start(f32[1,512]{1,0:T(1,128)} %param.30) | copy-start | bytes 6148
  0.7 5.0 %copy-start.2 = (f32[1,54,128]{2,0,1:T(1,128)S(1)}, f32[1,54,128]{2,0,1:T(1,128)}, u32[]{:S(2)}) copy-start(f32[1,54,128]{2,0,1:T(1,128)} %param.29) | copy-start | bytes 82948
  0.7 5.0 %copy-start.4 = (f32[1,512]{1,0:T(1,128)S(1)}, f32[1,512]{1,0:T(1,128)}, u32[]{:S(2)}) copy-start(f32[1,512]{1,0:T(1,128)} %param.27) | copy-start | bytes 6148
  0.7 5.0 %copy-start.1 = (f32[1,54,128]{2,0,1:T(1,128)S(1)}, f32[1,54,128]{2,0,1:T(1,128)}, u32[]{:S(2)}) copy-start(f32[1,54,128]{2,0,1:T(1,128)} %param.26) | copy-start | bytes 82948
  0.7 5.0 %copy-start = (f32[1,2,512,512]{3,2,1,0:T(8,128)S(1)}, f32[1,2,512,512]{3,2,1,0:T(8,128)}, u32[]{:S(2)}) copy-start(f32[1,2,512,512]{3,2,1,0:T(8,128)} %param.25) | copy-start | bytes 6291460
  0.7 5.0 %copy-start.7 = (s32[2,1]{0,1:T(1,128)S(1)}, s32[2,1]{0,1:T(1,128)}, u32[]{:S(2)}) copy-start(s32[2,1]{0,1:T(1,128)} %param.23) | copy-start | bytes 28
  0.7 5.0 %copy-start.8 = (s32[2,1,4]{2,1,0:T(1,128)S(1)}, s32[2,1,4]{2,1,0:T(1,128)}, u32[]{:S(2)}) copy-start(s32[2,1,4]{2,1,0:T(1,128)} %param.22) | copy-start | bytes 100
